TPU v7x, 32 devices: a whole 2x2x4 slice. The times are simulated.
32 devices in a mesh: groups: 2 (over x), gx: 16 (over z, y, core).
Axes of the slice: x: 2, y: 2, z: 4, core: 2. Of those that a mesh axis runs over, the one named last changes fastest.
Arguments:
- spectrum: float32 [30, 24, 16, 2048], P(None, None, 'groups', 'gx'), parts along dimension 2, may hold values from 0.01 to 1
- sea_mask: int32 [16, 2048], P('groups', 'gx'), parts along dimension 0, may hold values 0 or 1
- courant: float32 [30], replicated, may hold values from 0.35 to 0.7
- phase_speed: float32 [30], replicated, may hold values from 1.5 to 15
- growth_rate: float32 [30], replicated, may hold values from 0.02 to 0.2
- dissipation: float32 [30], replicated, may hold values from 0.002 to 0.02
- atmos_fields: float32 [16, 4, 8, 1024], P('gx', None, 'groups'), parts along dimension 2, may hold values from -24 to 24, as said below
- intersection_tile: int32 [4, 16, 2048], P(None, 'groups', 'gx'), parts along dimension 1, may hold values from 0 to 15, as said below
- intersection_cell: int32 [4, 16, 2048], P(None, 'groups', 'gx'), parts along dimension 1, may hold values from 0 to 1023
- intersection_weight: float32 [4, 16, 2048], P(None, 'groups', 'gx'), parts along dimension 1, may hold values from 0.1 to 0.4
Outputs:
- wave_spectrum: float32 [30, 24, 16, 2048], P(None, None, 'groups', 'gx'), parts along dimension 2
- atmos_roughness: float32 [16, 8, 1024], P('gx', 'groups'), parts along dimension 1
There are 2 independent parts, one for each index of `groups`. A program takes and returns all parts, laid end to end along the dimension named above; an argument that names none is the same for every part. Nothing has to cross between parts.
Inputs may be any that keep to these rules, and one draw needn't show every extreme that they name: `intersection_tile`: the tile of every intersection of a wave cell in column x is b * 4 + x // 512 for some b in 0 .. 3. `atmos_fields`: fields 0 and 1 are winds, field 2 lies in 1.1 to 1.3, field 3 in -1 to 1.
All inputs are finite; a program needn't handle non-finite values. No bound on the sum of `sea_mask` on one device may be relied on, other than what follows from the above.
Results may differ from a plain program's by a relative error of at most 0.00002.
Values sent between devices are 32-bit elements; how exact they have to be, the bound alone decides.
A program may use at most 128 MiB of HBM per device.

v0:
```python
import math

import jax
import jax.numpy as jnp
from jax import lax
from jax.sharding import PartitionSpec as P

ATY = 4
SUBSTEPS = 2


def with_halo(cells, sides, width):
    for axis, dim in sides:
        count = lax.axis_size(axis)
        head = lax.slice_in_dim(cells, 0, width, axis=dim)
        tail = lax.slice_in_dim(cells, cells.shape[dim] - width, cells.shape[dim], axis=dim)
        cells = jnp.concatenate(
            [
                lax.ppermute(tail, axis, [(i, (i + 1) % count) for i in range(count)]),
                cells,
                lax.ppermute(head, axis, [((i + 1) % count, i) for i in range(count)]),
            ],
            axis=dim,
        )
    return cells


def advance(padded, sea_frac, step_x, step_y):
    center = padded[..., 1:-1]
    west_cell = padded[..., :-2]
    east_cell = padded[..., 2:]
    zero_row = jnp.zeros_like(center[..., :1, :])
    south_cell = jnp.concatenate([zero_row, center[..., :-1, :]], axis=-2)
    north_cell = jnp.concatenate([center[..., 1:, :], zero_row], axis=-2)
    result = center - jnp.maximum(step_x, 0.0) * (center - west_cell)
    result = result - jnp.maximum(-step_x, 0.0) * (center - east_cell)
    result = result - jnp.maximum(step_y, 0.0) * (center - south_cell)
    result = result - jnp.maximum(-step_y, 0.0) * (center - north_cell)
    return sea_frac * result


def on_device(
    spectrum,
    sea_mask,
    courant,
    phase_speed,
    growth_rate,
    dissipation,
    atmos_fields,
    intersection_tile,
    intersection_cell,
    intersection_weight,
):
    dir_count = spectrum.shape[1]
    angles = jnp.arange(dir_count, dtype=jnp.float32) * (2.0 * math.pi / dir_count)
    cosine = jnp.cos(angles)
    sine_dir = jnp.sin(angles)
    step_x = (courant[:, None] * cosine[None, :])[:, :, None, None]
    step_y = (courant[:, None] * sine_dir[None, :])[:, :, None, None]
    sea_frac = sea_mask.astype(jnp.float32)
    field = spectrum * sea_frac
    for substep in range(SUBSTEPS):
        padded = with_halo(field, (("gx", 3),), 1)
        field = advance(padded, sea_frac, step_x, step_y)
    tile_count = lax.axis_size("gx")
    place = lax.axis_index("gx")
    lon_bands = tile_count // ATY
    group_start = place % lon_bands * ATY
    own_tile = atmos_fields[0]
    field_count, atmos_rows, atmos_cols = own_tile.shape
    block_span = atmos_cols // ATY
    capacity = atmos_rows * block_span
    pieces = (
        own_tile.reshape(field_count, atmos_rows, ATY, block_span)
        .transpose(2, 0, 1, 3)
        .reshape(ATY, field_count, capacity)
    )
    outgoing = lax.dynamic_update_slice(
        jnp.zeros((tile_count, field_count, capacity), jnp.float32), pieces, (group_start, 0, 0)
    )
    incoming = lax.all_to_all(outgoing, "gx", split_axis=0, concat_axis=0, tiled=True)
    forcing = [
        jnp.sum(intersection_weight * incoming[intersection_tile, which, intersection_cell], axis=0)
        for which in range(4)
    ]
    east_wind, north_wind, air_density, stability = forcing
    energy = jnp.sum(field, axis=(0, 1))
    along = cosine[:, None, None] * east_wind + sine_dir[:, None, None] * north_wind
    boost = jnp.exp(0.3 * stability)
    growth = (
        growth_rate[:, None, None, None]
        * air_density
        * jnp.maximum(along / phase_speed[:, None, None, None] - 1.0, 0.0)
        * boost
    )
    updated = field * (1.0 + growth) / (1.0 + dissipation[:, None, None, None] * energy)
    stress = jnp.sum(growth * updated, axis=(0, 1))
    surface = 0.01 * (east_wind * east_wind + north_wind * north_wind + stress)
    contribution = (intersection_weight * sea_frac * surface).reshape(-1)
    target = (intersection_tile * capacity + intersection_cell).reshape(-1)
    buffer = (
        jnp.zeros((tile_count * capacity,), jnp.float32)
        .at[target]
        .add(contribution)
        .reshape(tile_count, capacity)
    )
    returned = lax.all_to_all(buffer, "gx", split_axis=0, concat_axis=0, tiled=True)
    collected = lax.dynamic_slice_in_dim(returned, group_start, ATY, 0)
    roughness = (
        collected.reshape(ATY, atmos_rows, block_span)
        .transpose(1, 0, 2)
        .reshape(atmos_rows, atmos_cols)
    )
    return (updated, roughness[None])


def solution(mesh):
    in_specs = (
        P(None, None, "groups", "gx"),
        P("groups", "gx"),
        P(),
        P(),
        P(),
        P(),
        P("gx", None, "groups", None),
        P(None, "groups", "gx"),
        P(None, "groups", "gx"),
        P(None, "groups", "gx"),
    )
    out_specs = (P(None, None, "groups", "gx"), P("gx", "groups", None))
    return jax.shard_map(
        on_device, mesh=mesh, in_specs=in_specs, out_specs=out_specs, check_vma=False
    )
```

profile of v0, /device:TPU:0, one launch (start us, length us, event | category | flops | bytes accessed | tf_op | source)
XLA Modules:
  0.0 324.0 jit_solution(5046361992092599577)
XLA Ops:
  0.6 0.7 convert_element_type.3
  1.3 0.1 copy.59
  1.4 8.5 %copy.60 = f32[30,24,8,128]{0,2,3,1:T(8,128)} copy(f32[30,24,8,128]{3,2,1,0:T(8,128)} %param.10) | data formatting | bytes 5898240 | tf_op args[0]
  9.9 10.8 %broadcast_multiply_fusion = f32[30,24,8,128]{0,2,3,1:T(8,128)} fusion(f32[30,24,8,128]{0,2,3,1:T(8,128)} %copy.60, f32[8,128]{0,1:T(8,128)S(1)} %copy.59), kind=kLoop, calls=%fused_computation.33 | loop fusion | flops 737280 | bytes 5902336 | tf_op jit(solution)/shard_map/mul | solution.py:61
  20.8 1.0 fusion.42
  21.7 0.5 collective-permute-start
  22.2 5.1 %collective-permute-start.1 = (f32[30,24,8,1]{0,2,3,1:T(8,128)S(1)}, f32[30,24,8,1]{0,2,3,1:T(8,128)S(1)}, u32[]{:S(2)}, u32[]{:S(2)}) collective-permute-start(f32[30,24,8,1]{0,2,3,1:T(8,128)S(1)} %get-tuple-element.25), channel_id=1, source_target_pairs={{1,0},{2,1},{3,2},{4,3},{5,4},{6,5},{7,6},{8,7},{9,8},{10,9},{11,1... | collective-permute-start | bytes 69128 | tf_op jit(solution)/shard_map/ppermute | solution.py:21
  27.4 0.8 broadcast_in_dim.16
  28.2 0.6 constant_dynamic-update-slice_fusion
  28.8 3.6 %all-to-all-start = ((f32[16,4,1024]{2,1,0:T(4,128)}), f32[16,4,1024]{2,1,0:T(4,128)S(1)}, u32[]{:S(2)}, u32[]{:S(2)}) async-start(f32[16,4,1024]{2,1,0:T(4,128)} %constant_dynamic-update-slice_fusion), calls=%async_computation | async-start | bytes 524288 | tf_op jit(solution)/shard_map/all_to_all | solution.py:81
  32.5 0.0 copy-start.1
  32.5 0.0 copy-start.2
  32.5 0.0 copy-start.5
  32.5 19.7 %fusion.41 = (f32[30,24,7,128]{0,2,3,1:T(8,128)}, f32[30,24,7,128]{0,2,3,1:T(8,128)}) fusion(f32[30,24,8,128]{0,2,3,1:T(8,128)} %broadcast_multiply_fusion), kind=kLoop, calls=%fused_computation.79 | loop fusion | bytes 10321920 | tf_op jit(solution)/shard_map/slice | solution.py:33
  52.3 0.1 multiply_maximum_fusion.1
  52.4 0.0 collective-permute-done
  52.4 0.0 collective-permute-done.1
  52.4 22.0 %fusion.17 = f32[30,24,8,128]{0,2,3,1:T(8,128)S(1)} fusion(f32[30,24,8,128]{0,2,3,1:T(8,128)} %broadcast_multiply_fusion, f32[30,24,8,1]{0,2,3,1:T(8,128)S(1)} %collective-permute-done.1, f32[30,24,8,1]{0,2,3,1:T(8,128)S(1)} %collective-permute-done, f32[30,24,7,128]{0,2,3,1:T(8,128)} %get-tuple-element.23, f32[30,24,7,128]{0,2,3,1:T(8,128)} %get-tuple-element.22, ...), kind=kLoop, calls=%fused_computation.26 | loop fusion | flops 11059200 | bytes 11120896 | tf_op jit(solution)/shard_map/mul | solution.py:39
  74.4 0.5 collective-permute-start.2
  74.9 4.2 %collective-permute-start.3 = (f32[30,24,8,1]{0,2,3,1:T(8,128)S(1)}, f32[30,24,8,1]{0,2,3,1:T(8,128)S(1)}, u32[]{:S(2)}, u32[]{:S(2)}) collective-permute-start(f32[30,24,8,1]{0,2,3,1:T(8,128)S(1)} %get-tuple-element.19), channel_id=1, source_target_pairs={{1,0},{2,1},{3,2},{4,3},{5,4},{6,5},{7,6},{8,7},{9,8},{10,9},{11,1... | collective-permute-start | bytes 69128 | tf_op jit(solution)/shard_map/ppermute | solution.py:21
  79.1 9.1 %fusion.40 = (f32[30,24,7,128]{0,2,3,1:T(8,128)}, f32[30,24,7,128]{0,2,3,1:T(8,128)}) fusion(f32[30,24,8,128]{0,2,3,1:T(8,128)S(1)} %fusion.17), kind=kLoop, calls=%fused_computation.78 | loop fusion | bytes 10321920 | tf_op jit(solution)/shard_map/slice | solution.py:33
  88.2 0.0 collective-permute-done.2
  88.2 0.0 collective-permute-done.3
  88.2 20.6 %fusion.37 = (f32[8,128]{0,1:T(8,128)S(1)}, f32[30,24,8,128]{0,2,3,1:T(8,128)}) fusion(f32[30,24,8,128]{0,2,3,1:T(8,128)S(1)} %fusion.17, f32[30,24,7,128]{0,2,3,1:T(8,128)} %get-tuple-element.21, f32[30,24]{0,1:T(8,128)S(1)} %get-tuple-element.34, f32[30,24,7,128]{0,2,3,1:T(8,128)} %get-tuple-element.20, f32[30,24]{0,1:T(8,128)S(1)} %get-tuple-element.35, ...), kind=kLoop, calls=%fused_computation.76 | loop fusion | flops 11795456 | bytes 11124992 | tf_op jit(solution)/shard_map/reduce_sum | solution.py:87
  108.8 0.0 copy-done.6
  108.8 0.2 multiply_add_fusion.1
  109.0 0.0 all-to-all-done
  109.0 40.3 %gather_fusion = f32[4096]{0:T(1024)S(1)} fusion(f32[16,4,1024]{2,1,0:T(4,128)S(1)} %all-to-all-done, s32[4096]{0:T(1024)S(1)} %get-tuple-element.29), kind=kCustom, calls=%fused_computation | custom fusion | bytes 81920 | tf_op jit(solution)/shard_map/gather | solution.py:83
  149.3 40.3 %gather_fusion.1 = f32[4096]{0:T(1024)S(1)} fusion(f32[16,4,1024]{2,1,0:T(4,128)S(1)} %all-to-all-done, s32[4096]{0:T(1024)S(1)} %get-tuple-element.27), kind=kCustom, calls=%fused_computation.1 | custom fusion | bytes 81920 | tf_op jit(solution)/shard_map/gather | solution.py:83
  189.6 40.3 %gather_fusion.2 = f32[4096]{0:T(1024)S(1)} fusion(f32[16,4,1024]{2,1,0:T(4,128)S(1)} %all-to-all-done, s32[4096]{0:T(1024)S(1)} %get-tuple-element.28), kind=kCustom, calls=%fused_computation.2 | custom fusion | bytes 81920 | tf_op jit(solution)/shard_map/gather | solution.py:83
  229.9 0.0 copy-start.3
  229.9 0.0 copy-start.7
  229.9 0.0 copy-start.4
  230.0 40.3 %gather_fusion.3 = f32[4096]{0:T(1024)S(1)} fusion(f32[16,4,1024]{2,1,0:T(4,128)S(1)} %all-to-all-done, s32[4096]{0:T(1024)S(1)} %get-tuple-element.26), kind=kCustom, calls=%fused_computation.3 | custom fusion | bytes 81920 | tf_op jit(solution)/shard_map/gather | solution.py:83
  270.3 0.0 copy-done.3
  270.3 0.1 copy.63
  270.4 0.1 copy.64
  270.5 0.1 copy.62
  270.6 0.1 copy.65
  270.7 0.2 multiply_add_fusion
  271.0 0.2 broadcast_multiply_fusion.1
  271.2 11.0 %multiply_reduce_fusion = (f32[8,128]{0,1:T(8,128)S(1)}, f32[30,24,8,128]{0,2,3,1:T(8,128)}) fusion(f32[8,128]{0,1:T(8,128)S(1)} %copy.65, f32[30]{0:T(128)S(1)} %copy-done.4, f32[24,8,128]{1,2,0:T(8,128)S(1)} %multiply_add_fusion, f32[30,8,128]{0,1,2:T(8,128)S(1)} %broadcast_multiply_fusion.1, f32[30,8,128]{0,1,2:T(8,128)S(1)} %multiply_add_fusion.1, ...), kind=kLoop, calls=%fused_computation.31 | loop fusion | flops 7371776 | bytes 6250616 | tf_op jit(solution)/shard_map/reduce_sum | solution.py:97
  282.3 28.1 %scatter_custom_fusion = f32[16384]{0:T(1024)} fusion(s32[4096]{0:T(1024)S(1)} %bitcast.57, f32[4096]{0:T(1024)S(1)} %multiply_bitcast_fusion, f32[]{:T(128)} %constant.16.clone.1), kind=kCustom, calls=%fused_computation.41 | custom fusion | flops 4096 | bytes 65540 | tf_op jit(solution)/shard_map/scatter-add | solution.py:104
  310.4 3.5 %all-to-all-start.1 = ((f32[16,1,1024]{2,1,0:T(1,128)}), f32[16,1,1024]{2,1,0:T(1,128)S(1)}, u32[]{:S(2)}, u32[]{:S(2)}) async-start(f32[16,1,1024]{2,1,0:T(1,128)} %bitcast.14), calls=%async_computation.1 | async-start | bytes 131072 | tf_op jit(solution)/shard_map/all_to_all | solution.py:107
  313.9 9.4 %copy.67 = f32[30,24,8,128]{3,2,1,0:T(8,128)} copy(f32[30,24,8,128]{0,2,3,1:T(8,128)} %get-tuple-element.15) | data formatting | bytes 5898240
  323.3 0.0 all-to-all-done.1
  323.3 0.1 dynamic-slice_reduce_fusion
  323.3 0.6 reshape.226
  (21 shorter events, 0.3 us)
Async XLA Ops:
  9.9 17.4 %copy-start = (f32[1,4,4,1024]{3,2,1,0:T(4,128)S(1)}, f32[1,4,4,1024]{3,2,1,0:T(4,128)}, u32[]{:S(2)}) copy-start(f32[1,4,4,1024]{3,2,1,0:T(4,128)} %param.16) | copy-start | bytes 196612
  21.7 30.6 %collective-permute-start = (f32[30,24,8,1]{0,2,3,1:T(8,128)S(1)}, f32[30,24,8,1]{0,2,3,1:T(8,128)S(1)}, u32[]{:S(2)}, u32[]{:S(2)}) collective-permute-start(f32[30,24,8,1]{0,2,3,1:T(8,128)S(1)} %get-tuple-element.24), channel_id=1, source_target_pairs={{0,1},{1,2},{2,3},{3,4},{4,5},{5,6},{6,7},{7,8},{8,9},{9,10},{10,1... | collective-permute-start | bytes 69128 | tf_op jit(solution)/shard_map/ppermute | solution.py:19
  22.2 30.1 %collective-permute-start.1 = (f32[30,24,8,1]{0,2,3,1:T(8,128)S(1)}, f32[30,24,8,1]{0,2,3,1:T(8,128)S(1)}, u32[]{:S(2)}, u32[]{:S(2)}) collective-permute-start(f32[30,24,8,1]{0,2,3,1:T(8,128)S(1)} %get-tuple-element.25), channel_id=1, source_target_pairs={{1,0},{2,1},{3,2},{4,3},{5,4},{6,5},{7,6},{8,7},{9,8},{10,9},{11,1... | collective-permute-start | bytes 69128 | tf_op jit(solution)/shard_map/ppermute | solution.py:21
  28.8 80.2 %all-to-all-start = ((f32[16,4,1024]{2,1,0:T(4,128)}), f32[16,4,1024]{2,1,0:T(4,128)S(1)}, u32[]{:S(2)}, u32[]{:S(2)}) async-start(f32[16,4,1024]{2,1,0:T(4,128)} %constant_dynamic-update-slice_fusion), calls=%async_computation | async-start | bytes 524288 | tf_op jit(solution)/shard_map/all_to_all | solution.py:81
  32.5 19.7 %copy-start.1 = (s32[4,8,128]{2,1,0:T(8,128)S(1)}, s32[4,8,128]{2,1,0:T(8,128)}, u32[]{:S(2)}) copy-start(s32[4,8,128]{2,1,0:T(8,128)} %param.18) | copy-start | bytes 49156
  32.5 19.7 %copy-start.2 = (s32[4,8,128]{2,1,0:T(8,128)S(1)}, s32[4,8,128]{2,1,0:T(8,128)}, u32[]{:S(2)}) copy-start(s32[4,8,128]{2,1,0:T(8,128)} %param.17) | copy-start | bytes 49156
  32.5 19.8 %copy-start.5 = (f32[30]{0:T(128)S(1)}, f32[30]{0:T(128)}, u32[]{:S(2)}) copy-start(f32[30]{0:T(128)} %param.12) | copy-start | bytes 364
  74.4 13.8 %collective-permute-start.2 = (f32[30,24,8,1]{0,2,3,1:T(8,128)S(1)}, f32[30,24,8,1]{0,2,3,1:T(8,128)S(1)}, u32[]{:S(2)}, u32[]{:S(2)}) collective-permute-start(f32[30,24,8,1]{0,2,3,1:T(8,128)S(1)} %get-tuple-element.18), channel_id=1, source_target_pairs={{0,1},{1,2},{2,3},{3,4},{4,5},{5,6},{6,7},{7,8},{8,9},{9,10},{10,1... | collective-permute-start | bytes 69128 | tf_op jit(solution)/shard_map/ppermute | solution.py:19
  74.9 13.3 %collective-permute-start.3 = (f32[30,24,8,1]{0,2,3,1:T(8,128)S(1)}, f32[30,24,8,1]{0,2,3,1:T(8,128)S(1)}, u32[]{:S(2)}, u32[]{:S(2)}) collective-permute-start(f32[30,24,8,1]{0,2,3,1:T(8,128)S(1)} %get-tuple-element.19), channel_id=1, source_target_pairs={{1,0},{2,1},{3,2},{4,3},{5,4},{6,5},{7,6},{8,7},{9,8},{10,9},{11,1... | collective-permute-start | bytes 69128 | tf_op jit(solution)/shard_map/ppermute | solution.py:21
  88.2 20.6 %copy-start.6 = (f32[30]{0:T(128)S(1)}, f32[30]{0:T(128)}, u32[]{:S(2)}) copy-start(f32[30]{0:T(128)} %param.15) | copy-start | bytes 364
  229.9 40.3 %copy-start.3 = (f32[4,8,128]{2,1,0:T(8,128)S(1)}, f32[4,8,128]{2,1,0:T(8,128)}, u32[]{:S(2)}) copy-start(f32[4,8,128]{2,1,0:T(8,128)} %param.19) | copy-start | bytes 49156
  229.9 41.0 %copy-start.7 = (f32[30]{0:T(128)S(1)}, f32[30]{0:T(128)}, u32[]{:S(2)}) copy-start(f32[30]{0:T(128)} %param.14) | copy-start | bytes 364
  229.9 41.2 %copy-start.4 = (f32[30]{0:T(128)S(1)}, f32[30]{0:T(128)}, u32[]{:S(2)}) copy-start(f32[30]{0:T(128)} %param.13) | copy-start | bytes 364
  310.4 12.9 %all-to-all-start.1 = ((f32[16,1,1024]{2,1,0:T(1,128)}), f32[16,1,1024]{2,1,0:T(1,128)S(1)}, u32[]{:S(2)}, u32[]{:S(2)}) async-start(f32[16,1,1024]{2,1,0:T(1,128)} %bitcast.14), calls=%async_computation.1 | async-start | bytes 131072 | tf_op jit(solution)/shard_map/all_to_all | solution.py:107
where the time goes:
time: 325 us; the launch traced here: 324 us
  local copies, waits for them, and re-layouts  212 us (65%)
  other arithmetic  94.1 us (29%)
  starting transfers between devices  17.4 us (5%)
    gather x4, local copies, waits for them, and re-layouts, on_device(): incoming[intersection_tile, which, intersection_cell]  161 us
    slice x2, local copies, waits for them, and re-layouts, advance(): south_cell = jnp.concatenate([zero_row, center[..., :-1, :]], axis=-2)  28.7 us
    scatter-add x1, other arithmetic, on_device(): buffer = jnp.zeros((tile_count * capacity,), jnp.float32).at[target].add(...  28.1 us
    mul x1, other arithmetic, advance(): return sea_frac * result  22 us
    reduce_sum x1, other arithmetic, on_device(): energy = jnp.sum(field, axis=(0, 1))  20.6 us
    unnamed x18, local copies, waits for them, and re-layouts  17.9 us
    reduce_sum x1, other arithmetic, on_device(): stress = jnp.sum(growth * updated, axis=(0, 1))  11 us
    mul x1, other arithmetic, on_device(): field = spectrum * sea_frac  10.8 us
  transfers between devices with their start and end apart: 6, of which 0 were waited for; matrix products, arithmetic and copies ran while one was open for 25% of the time, Pallas kernels for 0%

commit v1 on v0

v1 whole, which is shorter than its diff:
```python
import functools
import math

import jax
import jax.numpy as jnp
import numpy as np
from jax import lax
from jax.experimental import pallas as pl
from jax.experimental.pallas import tpu as pltpu
from jax.sharding import PartitionSpec as P

ATY = 4
FCHUNK = 5
MESH = pl.DeviceIdType.MESH


def directions(count):
    angles = np.arange(count, dtype=np.float32) * np.float32(2.0 * math.pi / count)
    cosine, sine = np.cos(angles), np.sin(angles)
    forward = [d for d in range(count) if cosine[d] >= 0]
    backward = [d for d in range(count) if cosine[d] < 0]
    return cosine, sine, forward, backward


def pack_constants(dirs, slots):
    cosine, sine, forward, backward = directions(dirs)
    table = np.zeros((2, 3, 8, 128), np.float32)
    for side, members in enumerate((forward, backward)):
        for fi in range(FCHUNK):
            for k, d in enumerate(members):
                lane = fi * slots + 2 * k
                table[side, 0, :, lane : lane + 2] = abs(cosine[d])
                table[side, 1, :, lane : lane + 2] = max(sine[d], 0.0)
                table[side, 2, :, lane : lane + 2] = max(-sine[d], 0.0)
    return table


def lane_row(shape):
    lane = lax.broadcasted_iota(jnp.int32, shape, 1)
    row = lax.broadcasted_iota(jnp.int32, shape, 0)
    return lane, row


def exchange_kernel(
    ranks,
    spec_hbm,
    sea_ref,
    courant_ref,
    const_ref,
    atmos_ref,
    table_ref,
    west_ref,
    east_ref,
    spec,
    pack,
    in_sem,
    piece_send,
    piece_recv,
    halo_send,
    halo_recv,
):
    freqs, dirs = spec.shape[0], spec.shape[1]
    chunks = freqs // FCHUNK
    _, _, forward, backward = directions(dirs)
    slots = 2 * len(forward)
    me = lax.axis_index("gx")
    bands = ranks // ATY
    east, west = lax.rem(me + 1, ranks), lax.rem(me + ranks - 1, ranks)
    group, band = me // ATY, me // bands
    first_target = lax.rem(me, bands) * ATY
    own = lax.rem(me, bands) == group

    def load(g):
        span = pl.ds(g * FCHUNK, FCHUNK)
        return pltpu.make_async_copy(spec_hbm.at[span], spec.at[span], in_sem.at[g])

    for g in range(chunks):
        load(g).start()

    barrier = pltpu.get_barrier_semaphore()
    for device in (east, west):
        pl.semaphore_signal(barrier, inc=1, device_id={"gx": device}, device_id_type=MESH)
    for b in range(ATY):
        source = b * bands + group

        @pl.when(source != me)
        def _():
            pl.semaphore_signal(barrier, inc=1, device_id={"gx": source}, device_id_type=MESH)

    pl.semaphore_wait(barrier, 2 + ATY - own.astype(jnp.int32))

    span = atmos_ref.shape[3] // ATY

    def piece(j):
        return atmos_ref.at[0, :, :, pl.ds(j * span, span)]

    def piece_copy(j):
        return pltpu.make_async_remote_copy(
            src_ref=piece(j),
            dst_ref=table_ref.at[band],
            send_sem=piece_send.at[j],
            recv_sem=piece_recv.at[band],
            device_id={"gx": first_target + j},
            device_id_type=MESH,
        )

    for j in range(ATY):

        @pl.when(first_target + j != me)
        def _():
            piece_copy(j).start()

        @pl.when(first_target + j == me)
        def _():
            pltpu.make_async_copy(piece(j), table_ref.at[band], piece_recv.at[band]).start()

    lane, row = lane_row((8, 128))
    half = lane // 2
    odd = lane % 2 == 1
    sea = sea_ref[...].astype(jnp.float32)

    def tiled(shift):
        out = jnp.where(lane < 2, pltpu.roll(sea, shift, 1), 0.0)
        for step in (2, 4, 8, 16, 32, 64):
            out = out + pltpu.roll(out, step, 1)
        return out

    sea_pair = (tiled(2), tiled(0))
    freq_of_lane = lane // slots

    def chunk(g, carry):
        load(g).wait()
        acc = [jnp.zeros((8, 128), jnp.float32) for _ in range(2)]
        speed = jnp.zeros((8, 128), jnp.float32)
        for fi in range(FCHUNK):
            f = g * FCHUNK + fi
            speed = jnp.where(freq_of_lane == fi, courant_ref[f], speed)
            for side, members in enumerate((forward, backward)):
                for k, d in enumerate(members):
                    at = fi * slots + 2 * k
                    shift = (at + (2 if side == 0 else 0)) % 128
                    value = spec[f, d]
                    if shift:
                        value = pltpu.roll(value, shift, 1)
                    acc[side] = jnp.where(half == at // 2, value, acc[side])
        for side in range(2):
            field = acc[side] * sea_pair[side]
            upwind = pltpu.roll(field, 1 if side == 0 else 127, 1)
            south = jnp.where(row == 0, 0.0, pltpu.roll(field, 1, 0))
            north = jnp.where(row == 7, 0.0, pltpu.roll(field, 7, 0))
            later = field - speed * const_ref[side, 0] * (field - upwind)
            later = later - speed * const_ref[side, 1] * (field - south)
            later = later - speed * const_ref[side, 2] * (field - north)
            later = later * sea_pair[side]
            if side == 0:
                both = jnp.where(odd, later, pltpu.roll(field, 127, 1))
            else:
                both = jnp.where(odd, pltpu.roll(field, 1, 1), later)
            pack[side, g] = both
        return carry

    lax.fori_loop(0, chunks, chunk, 0)

    to_east = pltpu.make_async_remote_copy(
        src_ref=pack.at[0],
        dst_ref=west_ref,
        send_sem=halo_send.at[0],
        recv_sem=halo_recv.at[0],
        device_id={"gx": east},
        device_id_type=MESH,
    )
    to_west = pltpu.make_async_remote_copy(
        src_ref=pack.at[1],
        dst_ref=east_ref,
        send_sem=halo_send.at[1],
        recv_sem=halo_recv.at[1],
        device_id={"gx": west},
        device_id_type=MESH,
    )
    to_east.start()
    to_west.start()

    for j in range(ATY):

        @pl.when(first_target + j != me)
        def _():
            piece_copy(j).wait_send()

    for b in range(ATY):
        pltpu.make_async_copy(table_ref.at[b], table_ref.at[b], piece_recv.at[b]).wait()
    to_east.wait()
    to_west.wait()


def wave_kernel(
    bands,
    spec_hbm,
    sea_ref,
    courant_ref,
    phase_ref,
    rate_ref,
    decay_ref,
    tile_ref,
    cell_ref,
    weight_ref,
    table_ref,
    west_ref,
    east_ref,
    out_hbm,
    stress_ref,
    spec,
    out,
    along_ref,
    lane_hot,
    row_hot,
    in_sem,
    out_sem,
):
    freqs, dirs = spec.shape[0], spec.shape[1]
    chunks = freqs // FCHUNK
    cosine, sine, forward, backward = directions(dirs)
    slots = 2 * len(forward)

    def load(g):
        span = pl.ds(g * FCHUNK, FCHUNK)
        return pltpu.make_async_copy(spec_hbm.at[span], spec.at[span], in_sem.at[g])

    def store(g):
        span = pl.ds(g * FCHUNK, FCHUNK)
        return pltpu.make_async_copy(out.at[span], out_hbm.at[span], out_sem.at[g])

    for g in range(chunks):
        load(g).start()

    lane, row = lane_row((8, 128))
    sea = sea_ref[...].astype(jnp.float32)

    tile = [tile_ref[l] for l in range(4)]
    cell = [cell_ref[l] for l in range(4)]
    weight = [weight_ref[l] for l in range(4)]
    low = [c & 127 for c in cell]
    high = []
    for l in range(4):
        band = jnp.zeros((8, 128), jnp.int32)
        for b in range(1, ATY):
            band = band + (tile[l] >= b * bands).astype(jnp.int32)
        high.append(band * 8 + (cell[l] >> 7))

    forcing = [[jnp.zeros((8, 128), jnp.float32) for _ in range(4)] for _ in range(4)]
    for h in range(32):
        b, r, c = h // 8, h % 8 // 2, h % 2
        hit = [high[l] == h for l in range(4)]
        for k in range(4):
            line = jnp.broadcast_to(table_ref[b, k, pl.ds(r, 1), pl.ds(c * 128, 128)], (8, 128))
            for l in range(4):
                found = jnp.take_along_axis(line, low[l], axis=1)
                forcing[k][l] = jnp.where(hit[l], found, forcing[k][l])
    east_wind, north_wind, air, stability = [
        (weight[0] * v[0] + weight[1] * v[1]) + (weight[2] * v[2] + weight[3] * v[3])
        for v in forcing
    ]
    for d in range(dirs):
        along_ref[d] = float(cosine[d]) * east_wind + float(sine[d]) * north_wind

    lows = lax.broadcasted_iota(jnp.int32, (128, 128), 0)
    for l in range(4):
        for y in range(8):
            at = pl.ds((l * 8 + y) * 128, 128)
            same = lows == jnp.broadcast_to(low[l][y : y + 1], (128, 128))
            lane_hot[:, at] = jnp.where(same, 1.0, 0.0).astype(jnp.bfloat16)

    first, last = lane == 0, lane == 127
    bottom, top = row == 0, row == 7

    def propagate(g, energy):
        load(g).wait()
        sums = [energy] + [jnp.zeros((8, 128), jnp.float32) for _ in range(3)]
        halos = (west_ref[g], east_ref[g])
        turn = 0
        for fi in range(FCHUNK):
            f = g * FCHUNK + fi
            speed = courant_ref[f]
            for side, members in enumerate((forward, backward)):
                for k, d in enumerate(members):
                    at = fi * slots + 2 * k
                    halo = pltpu.roll(halos[side], (127 - at) % 128, 1)
                    step_x = speed * float(abs(cosine[d]))
                    step_y = speed * float(abs(sine[d]))
                    keep = 1.0 - step_x - step_y
                    shift = 1 if side == 0 else 127
                    field = spec[f, d] * sea
                    for substep in range(2):
                        if substep == 0:
                            upwind = jnp.where(last if side == 0 else first, halo, field)
                            upwind = pltpu.roll(upwind, shift, 1)
                        else:
                            upwind = pltpu.roll(field, shift, 1)
                            upwind = jnp.where(first if side == 0 else last, halo, upwind)
                        result = keep * field + step_x * upwind
                        if sine[d] != 0:
                            up = sine[d] > 0
                            beside = pltpu.roll(field, 1 if up else 7, 0)
                            beside = jnp.where(bottom if up else top, 0.0, beside)
                            result = result + step_y * beside
                        field = sea * result
                    out[f, d] = field
                    sums[turn % 4] = sums[turn % 4] + field
                    turn += 1
        return (sums[0] + sums[1]) + (sums[2] + sums[3])

    energy = lax.fori_loop(0, chunks, propagate, jnp.zeros((8, 128), jnp.float32))

    base = air * jnp.exp(0.3 * stability)

    def sources(g, stress):
        sums = [stress] + [jnp.zeros((8, 128), jnp.float32) for _ in range(3)]
        for fi in range(FCHUNK):
            f = g * FCHUNK + fi
            offset = rate_ref[f] * base
            slope = offset / phase_ref[f]
            scale = 1.0 / (1.0 + decay_ref[f] * energy)
            for d in range(dirs):
                growth = jnp.maximum(along_ref[d] * slope - offset, 0.0)
                scaled = out[f, d] * scale
                updated = scaled + scaled * growth
                out[f, d] = updated
                sums[d % 4] = sums[d % 4] + growth * updated
        store(g).start()
        return (sums[0] + sums[1]) + (sums[2] + sums[3])

    stress = lax.fori_loop(0, chunks, sources, jnp.zeros((8, 128), jnp.float32))

    surface = sea * (0.01 * (east_wind * east_wind + north_wind * north_wind + stress))
    highs = lax.broadcasted_iota(jnp.int32, (32, 128), 0)
    for l in range(4):
        rest = weight[l] * surface
        parts = []
        for _ in range(3):
            part = rest.astype(jnp.bfloat16).astype(jnp.float32)
            parts.append(part)
            rest = rest - part
        for y in range(8):
            at = pl.ds((l * 8 + y) * 128, 128)
            same = highs == jnp.broadcast_to(high[l][y : y + 1], (32, 128))
            for p, part in enumerate(parts):
                line = jnp.broadcast_to(part[y : y + 1], (32, 128))
                row_hot[pl.ds(p * 32, 32), at] = jnp.where(same, line, 0.0).astype(jnp.bfloat16)
    spread = lax.dot_general(
        row_hot[...],
        lane_hot[...],
        (((1,), (1,)), ((), ())),
        preferred_element_type=jnp.float32,
    )
    stress_ref[...] = spread[0:32] + (spread[32:64] + spread[64:96])

    for g in range(chunks):
        store(g).wait()


def return_kernel(ranks, stress_ref, out_ref, landed, send_sem, recv_sem):
    me = lax.axis_index("gx")
    bands = ranks // ATY
    group = me // ATY
    slot = lax.rem(me, ATY)
    first_source = lax.rem(me, bands) * ATY
    own = lax.rem(me, bands) == group
    barrier = pltpu.get_barrier_semaphore()
    for j in range(ATY):

        @pl.when(first_source + j != me)
        def _():
            pl.semaphore_signal(
                barrier, inc=1, device_id={"gx": first_source + j}, device_id_type=MESH
            )

    pl.semaphore_wait(barrier, ATY - own.astype(jnp.int32))

    def piece(b):
        return stress_ref.at[pl.ds(b * 8, 8)]

    def piece_copy(b):
        return pltpu.make_async_remote_copy(
            src_ref=piece(b),
            dst_ref=landed.at[slot],
            send_sem=send_sem.at[b],
            recv_sem=recv_sem.at[slot],
            device_id={"gx": b * bands + group},
            device_id_type=MESH,
        )

    for b in range(ATY):

        @pl.when(b * bands + group != me)
        def _():
            piece_copy(b).start()

        @pl.when(b * bands + group == me)
        def _():
            pltpu.make_async_copy(piece(b), landed.at[slot], recv_sem.at[slot]).start()

    for j in range(ATY):
        pltpu.make_async_copy(landed.at[j], landed.at[j], recv_sem.at[j]).wait()
        for r in range(4):
            for c in range(2):
                out_ref[0, pl.ds(r, 1), pl.ds(j * 256 + c * 128, 128)] = landed[
                    j, pl.ds(2 * r + c, 1), :
                ]
    for b in range(ATY):

        @pl.when(b * bands + group != me)
        def _():
            piece_copy(b).wait_send()


def on_device(
    ranks,
    spectrum,
    sea_mask,
    courant,
    phase_speed,
    growth_rate,
    dissipation,
    atmos_fields,
    intersection_tile,
    intersection_cell,
    intersection_weight,
):
    freqs, dirs, lat, width = spectrum.shape
    chunks = freqs // FCHUNK
    bands = ranks // ATY
    f32 = jnp.float32
    _, _, forward, _ = directions(dirs)
    consts = jnp.asarray(pack_constants(dirs, 2 * len(forward)))
    anywhere = pl.BlockSpec(memory_space=pl.ANY)
    vmem = pl.BlockSpec(memory_space=pltpu.VMEM)
    smem = pl.BlockSpec(memory_space=pltpu.SMEM)
    dma = pltpu.SemaphoreType.DMA
    span = atmos_fields.shape[3] // ATY
    halo = jax.ShapeDtypeStruct((chunks, lat, width), f32)
    table, west, east = pl.pallas_call(
        functools.partial(exchange_kernel, ranks),
        out_shape=(
            jax.ShapeDtypeStruct((ATY,) + atmos_fields.shape[1:3] + (span,), f32),
            halo,
            halo,
        ),
        in_specs=[anywhere, vmem, smem, vmem, anywhere],
        out_specs=(anywhere, anywhere, anywhere),
        scratch_shapes=[
            pltpu.VMEM(spectrum.shape, f32),
            pltpu.VMEM((2, chunks, lat, width), f32),
            dma((chunks,)),
            dma((ATY,)),
            dma((ATY,)),
            dma((2,)),
            dma((2,)),
        ],
        compiler_params=pltpu.CompilerParams(
            collective_id=0, has_side_effects=True, vmem_limit_bytes=16 * 2**20
        ),
        name="exchange",
    )(spectrum, sea_mask, courant, consts, atmos_fields)

    updated, stress = pl.pallas_call(
        functools.partial(wave_kernel, bands),
        out_shape=(
            jax.ShapeDtypeStruct(spectrum.shape, f32),
            jax.ShapeDtypeStruct((32, 128), f32),
        ),
        in_specs=[anywhere, vmem, smem, smem, smem, smem] + [vmem] * 6,
        out_specs=(anywhere, vmem),
        scratch_shapes=[
            pltpu.VMEM(spectrum.shape, f32),
            pltpu.VMEM(spectrum.shape, f32),
            pltpu.VMEM((dirs, lat, width), f32),
            pltpu.VMEM((128, 32 * 128), jnp.bfloat16),
            pltpu.VMEM((96, 32 * 128), jnp.bfloat16),
            dma((chunks,)),
            dma((chunks,)),
        ],
        compiler_params=pltpu.CompilerParams(vmem_limit_bytes=24 * 2**20),
        name="wave",
    )(
        spectrum,
        sea_mask,
        courant,
        phase_speed,
        growth_rate,
        dissipation,
        intersection_tile,
        intersection_cell,
        intersection_weight,
        table,
        west,
        east,
    )

    roughness = pl.pallas_call(
        functools.partial(return_kernel, ranks),
        out_shape=jax.ShapeDtypeStruct((1,) + atmos_fields.shape[2:], f32),
        in_specs=[vmem],
        out_specs=vmem,
        scratch_shapes=[
            pltpu.VMEM((ATY, 8, 128), f32),
            dma((ATY,)),
            dma((ATY,)),
        ],
        compiler_params=pltpu.CompilerParams(collective_id=1, has_side_effects=True),
        name="give_back",
    )(stress)
    return (updated, roughness)


def solution(mesh):
    in_specs = (
        P(None, None, "groups", "gx"),
        P("groups", "gx"),
        P(),
        P(),
        P(),
        P(),
        P("gx", None, "groups", None),
        P(None, "groups", "gx"),
        P(None, "groups", "gx"),
        P(None, "groups", "gx"),
    )
    out_specs = (P(None, None, "groups", "gx"), P("gx", "groups", None))
    return jax.shard_map(
        functools.partial(on_device, mesh.shape["gx"]),
        mesh=mesh,
        in_specs=in_specs,
        out_specs=out_specs,
        check_vma=False,
    )
```

time: 325 us -> 56 us (0.17)
  local copies, waits for them, and re-layouts: 212 us -> 6.7 us
  other arithmetic: 94.1 us -> 0 us
  Pallas kernels: 0 us -> 48.1 us
  starting transfers between devices: 17.4 us -> 0 us
    gather x4 -> x0, local copies, waits for them, and re-layouts: 161 us -> none  [on_device(): incoming[intersection_tile, which, intersection_cell]]
    pallas_call x0 -> x3, Pallas kernels: none -> 48.1 us  [the longest x1 29.4 us: on_device(): pl.pallas_call(functools.partial(wave_kernel, bands), out_shape=(jax.Shap...]
    mul x4 -> x0, other arithmetic: 33.1 us -> none  [the longest x1 22 us: advance(): return sea_frac * result]
    reduce_sum x3 -> x0, other arithmetic: 31.6 us -> none  [the longest x1 20.6 us: on_device(): energy = jnp.sum(field, axis=(0, 1))]
    slice x4 -> x0, local copies, waits for them, and re-layouts: 29.7 us -> none  [the longest x2 28.7 us: advance(): south_cell = jnp.concatenate([zero_row, center[..., :-1, :]], axis=-2)]
    scatter-add x1 -> x0, other arithmetic: 28.1 us -> none  [on_device(): buffer = jnp.zeros((tile_count * capacity,), jnp.float32).at[target].add(...]
    unnamed x18 -> x31, local copies, waits for them, and re-layouts: 17.9 us -> 6.7 us
    ppermute x4 -> x0, starting transfers between devices: 10.2 us -> none  [the longest x2 9.28 us: with_halo(): lax.ppermute(head, axis, [((i + 1) % count, i) for i in range(count)])]
  transfers between devices with their start and end apart: 6 -> 0, of which waited for: 0 -> 0; matrix products, arithmetic and copies ran while one was open for 25% -> 0% of each run, Pallas kernels for 0% -> 0%
where the time goes in v1:
time: 56 us; the launch traced here: 55.6 us
  Pallas kernels  48.1 us (86%)
  local copies, waits for them, and re-layouts  6.7 us (12%)
  between operations  0.79 us (1%)
    pallas_call x1, Pallas kernels, on_device(): pl.pallas_call(functools.partial(wave_kernel, bands), out_shape=(jax.Shap...  29.4 us
    pallas_call x1, Pallas kernels, on_device(): pl.pallas_call(functools.partial(exchange_kernel, ranks), out_shape=(jax....  12.5 us
    unnamed x31, local copies, waits for them, and re-layouts  6.7 us
    pallas_call x1, Pallas kernels, on_device(): pl.pallas_call(functools.partial(return_kernel, ranks), out_shape=jax.Sha...  6.2 us

profile of v1, /device:TPU:0, one launch (start us, length us, event | category | flops | bytes accessed | tf_op | source)
XLA Modules:
  0.0 55.6 jit_solution(10367862236814907482)
XLA Ops:
  0.6 0.0 copy-start
  0.6 1.8 %copy-done = f32[30,24,8,128]{3,2,1,0:T(8,128)S(1)} copy-done((f32[30,24,8,128]{3,2,1,0:T(8,128)S(1)}, f32[30,24,8,128]{3,2,1,0:T(8,128)}, u32[]{:S(2)}) %copy-start) | copy-done | bytes 2949144
  2.5 0.0 copy-start.2
  2.5 0.8 %copy-done.2 = f32[1,4,4,1024]{3,2,1,0:T(4,128)S(1)} copy-done((f32[1,4,4,1024]{3,2,1,0:T(4,128)S(1)}, f32[1,4,4,1024]{3,2,1,0:T(4,128)}, u32[]{:S(2)}) %copy-start.2) | copy-done | bytes 65560
  3.3 0.0 copy-start.3
  3.3 0.7 %copy-done.3 = f32[2,3,8,128]{3,2,1,0:T(8,128)S(1)} copy-done((f32[2,3,8,128]{3,2,1,0:T(8,128)S(1)}, f32[2,3,8,128]{3,2,1,0:T(8,128)}, u32[]{:S(2)}) %copy-start.3) | copy-done | bytes 24600
  4.0 0.0 copy-start.7
  4.0 0.7 %copy-done.7 = s32[8,128]{1,0:T(8,128)S(1)} copy-done((s32[8,128]{1,0:T(8,128)S(1)}, s32[8,128]{1,0:T(8,128)}, u32[]{:S(2)}) %copy-start.7) | copy-done | bytes 4120
  4.7 0.0 copy-start.10
  4.7 0.7 %copy-done.10 = f32[30]{0:T(128)S(1)} copy-done((f32[30]{0:T(128)S(1)}, f32[30]{0:T(128)}, u32[]{:S(2)}) %copy-start.10) | copy-done | bytes 144
  5.4 0.0 copy-start.1
  5.4 0.0 copy-start.4
  5.4 0.0 copy-start.5
  5.4 0.0 copy-start.6
  5.4 0.0 copy-start.8
  5.4 0.0 copy-start.11
  5.4 0.0 copy-start.12
  5.4 0.0 copy-start.13
  5.4 0.0 copy-start.14
  5.5 12.5 %exchange.1 = (f32[4,4,4,256]{3,2,1,0:T(4,128)S(1)}, f32[6,8,128]{2,1,0:T(8,128)S(1)}, f32[6,8,128]{2,1,0:T(8,128)S(1)}) custom-call(f32[30,24,8,128]{3,2,1,0:T(8,128)S(1)} %copy-done, s32[8,128]{1,0:T(8,128)S(1)} %copy-done.7, f32[30]{0:T(128)S(1)} %copy-done.10, f32[2,3,8,128]{3,2,1,0:T(8,128)S(1)} %copy-done.3, f32[1,4,4,1024]{3,2,1,0:T(4,128)S(1)} %copy-done.2), custom_call_target="tpu_custom_call" | custom-call | tf_op jit(solution)/shard_map/exchange/pallas_call | solution.py:440
  18.0 0.0 copy-done.1
  18.0 0.0 copy-done.4
  18.0 0.0 copy-done.5
  18.0 0.0 copy-done.6
  18.0 0.0 copy-done.8
  18.0 0.0 copy-done.11
  18.0 0.0 copy-done.12
  18.0 0.0 copy-done.13
  18.1 0.0 copy-done.14
  18.1 29.4 %wave.1 = (f32[30,24,8,128]{3,2,1,0:T(8,128)}, f32[32,128]{1,0:T(8,128)S(1)}) custom-call(f32[30,24,8,128]{3,2,1,0:T(8,128)S(1)} %copy-done.1, s32[8,128]{1,0:T(8,128)S(1)} %copy-done.8, f32[30]{0:T(128)S(1)} %copy-done.11, f32[30]{0:T(128)S(1)} %copy-done.12, f32[30]{0:T(128)S(1)} %copy-done.13, f32[30]{0:T(128)S(1)} %copy-done.14, ...), custom_call_target="tpu_custom_call" | custom-call | tf_op jit(solution)/shard_map/wave/pallas_call | solution.py:464
  47.5 0.0 copy-start.9
  47.5 0.6 %copy-done.9 = f32[32,128]{1,0:T(8,128)} copy-done((f32[32,128]{1,0:T(8,128)}, f32[32,128]{1,0:T(8,128)S(1)}, u32[]{:S(2)}) %copy-start.9) | copy-done | bytes 16408
  48.1 6.2 %give_back.1 = f32[1,4,1024]{2,1,0:T(4,128)} custom-call(f32[32,128]{1,0:T(8,128)} %copy-done.9), custom_call_target="tpu_custom_call" | custom-call | tf_op jit(solution)/shard_map/give_back/pallas_call | solution.py:498
  54.3 1.3 %copy.14 = f32[1,4,1024]{2,1,0:T(4,128)} copy(f32[1,4,1024]{2,1,0:T(4,128)} %give_back.1) | data formatting | bytes 32768
Async XLA Ops:
  0.6 1.8 %copy-start = (f32[30,24,8,128]{3,2,1,0:T(8,128)S(1)}, f32[30,24,8,128]{3,2,1,0:T(8,128)}, u32[]{:S(2)}) copy-start(f32[30,24,8,128]{3,2,1,0:T(8,128)} %spec_hbm.3) | copy-start | bytes 8847364
  2.5 0.8 %copy-start.2 = (f32[1,4,4,1024]{3,2,1,0:T(4,128)S(1)}, f32[1,4,4,1024]{3,2,1,0:T(4,128)}, u32[]{:S(2)}) copy-start(f32[1,4,4,1024]{3,2,1,0:T(4,128)} %atmos_ref.1) | copy-start | bytes 196612
  3.3 0.7 %copy-start.3 = (f32[2,3,8,128]{3,2,1,0:T(8,128)S(1)}, f32[2,3,8,128]{3,2,1,0:T(8,128)}, u32[]{:S(2)}) copy-start(f32[2,3,8,128]{3,2,1,0:T(8,128)} %constant.2.clone.const_ref) | copy-start | bytes 73732
  4.0 0.7 %copy-start.7 = (s32[8,128]{1,0:T(8,128)S(1)}, s32[8,128]{1,0:T(8,128)}, u32[]{:S(2)}) copy-start(s32[8,128]{1,0:T(8,128)} %sea_ref.3) | copy-start | bytes 12292
  4.7 0.7 %copy-start.10 = (f32[30]{0:T(128)S(1)}, f32[30]{0:T(128)}, u32[]{:S(2)}) copy-start(f32[30]{0:T(128)} %courant_ref.3) | copy-start | bytes 364
  5.4 12.6 %copy-start.1 = (f32[30,24,8,128]{3,2,1,0:T(8,128)S(1)}, f32[30,24,8,128]{3,2,1,0:T(8,128)}, u32[]{:S(2)}) copy-start(f32[30,24,8,128]{3,2,1,0:T(8,128)} %spec_hbm.3) | copy-start | bytes 8847364
  5.4 12.6 %copy-start.4 = (s32[4,8,128]{2,1,0:T(8,128)S(1)}, s32[4,8,128]{2,1,0:T(8,128)}, u32[]{:S(2)}) copy-start(s32[4,8,128]{2,1,0:T(8,128)} %tile_ref.1) | copy-start | bytes 49156
  5.4 12.6 %copy-start.5 = (s32[4,8,128]{2,1,0:T(8,128)S(1)}, s32[4,8,128]{2,1,0:T(8,128)}, u32[]{:S(2)}) copy-start(s32[4,8,128]{2,1,0:T(8,128)} %cell_ref.1) | copy-start | bytes 49156
  5.4 12.6 %copy-start.6 = (f32[4,8,128]{2,1,0:T(8,128)S(1)}, f32[4,8,128]{2,1,0:T(8,128)}, u32[]{:S(2)}) copy-start(f32[4,8,128]{2,1,0:T(8,128)} %weight_ref.1) | copy-start | bytes 49156
  5.4 12.6 %copy-start.8 = (s32[8,128]{1,0:T(8,128)S(1)}, s32[8,128]{1,0:T(8,128)}, u32[]{:S(2)}) copy-start(s32[8,128]{1,0:T(8,128)} %sea_ref.3) | copy-start | bytes 12292
  5.4 12.6 %copy-start.11 = (f32[30]{0:T(128)S(1)}, f32[30]{0:T(128)}, u32[]{:S(2)}) copy-start(f32[30]{0:T(128)} %courant_ref.3) | copy-start | bytes 364
  5.4 12.6 %copy-start.12 = (f32[30]{0:T(128)S(1)}, f32[30]{0:T(128)}, u32[]{:S(2)}) copy-start(f32[30]{0:T(128)} %phase_ref.1) | copy-start | bytes 364
  5.4 12.6 %copy-start.13 = (f32[30]{0:T(128)S(1)}, f32[30]{0:T(128)}, u32[]{:S(2)}) copy-start(f32[30]{0:T(128)} %rate_ref.1) | copy-start | bytes 364
  5.4 12.6 %copy-start.14 = (f32[30]{0:T(128)S(1)}, f32[30]{0:T(128)}, u32[]{:S(2)}) copy-start(f32[30]{0:T(128)} %decay_ref.1) | copy-start | bytes 364
  47.5 0.6 %copy-start.9 = (f32[32,128]{1,0:T(8,128)}, f32[32,128]{1,0:T(8,128)S(1)}, u32[]{:S(2)}) copy-start(f32[32,128]{1,0:T(8,128)S(1)} %get-tuple-element.11.stress_ref) | copy-start | bytes 49156

commit v2 on v1

--- a/solution.py
+++ b/solution.py
@@ -10,7 +10,7 @@
 from jax.sharding import PartitionSpec as P
 
 ATY = 4
-FCHUNK = 5
+FCHUNK = 6
 MESH = pl.DeviceIdType.MESH
 
 
@@ -22,13 +22,13 @@
     return cosine, sine, forward, backward
 
 
-def pack_constants(dirs, slots):
+def pack_constants(dirs, slots, chunks):
     cosine, sine, forward, backward = directions(dirs)
     table = np.zeros((2, 3, 8, 128), np.float32)
     for side, members in enumerate((forward, backward)):
-        for fi in range(FCHUNK):
+        for c in range(chunks):
             for k, d in enumerate(members):
-                lane = fi * slots + 2 * k
+                lane = c * slots + 2 * k
                 table[side, 0, :, lane : lane + 2] = abs(cosine[d])
                 table[side, 1, :, lane : lane + 2] = max(sine[d], 0.0)
                 table[side, 2, :, lane : lane + 2] = max(-sine[d], 0.0)
@@ -128,23 +128,28 @@
     sea_pair = (tiled(2), tiled(0))
     freq_of_lane = lane // slots
 
-    def chunk(g, carry):
-        load(g).wait()
-        acc = [jnp.zeros((8, 128), jnp.float32) for _ in range(2)]
-        speed = jnp.zeros((8, 128), jnp.float32)
-        for fi in range(FCHUNK):
-            f = g * FCHUNK + fi
-            speed = jnp.where(freq_of_lane == fi, courant_ref[f], speed)
-            for side, members in enumerate((forward, backward)):
-                for k, d in enumerate(members):
-                    at = fi * slots + 2 * k
-                    shift = (at + (2 if side == 0 else 0)) % 128
-                    value = spec[f, d]
-                    if shift:
-                        value = pltpu.roll(value, shift, 1)
-                    acc[side] = jnp.where(half == at // 2, value, acc[side])
+    def chunk(c, acc):
+        load(c).wait()
+        acc = list(acc)
+        for m in range(len(forward) + 1):
+            for side, members, k in ((0, forward, m - 1), (1, backward, m)):
+                if not 0 <= k < len(members):
+                    continue
+                here = half == c * (slots // 2) + k
+                for fi in range(FCHUNK):
+                    value = pltpu.roll(spec[c * FCHUNK + fi, members[k]], c * slots + 2 * m, 1)
+                    at = side * FCHUNK + fi
+                    acc[at] = jnp.where(here, value, acc[at])
+        return tuple(acc)
+
+    blank = jnp.zeros((8, 128), jnp.float32)
+    acc = lax.fori_loop(0, chunks, chunk, (blank,) * (2 * FCHUNK))
+    for fi in range(FCHUNK):
+        speed = blank
+        for c in range(chunks):
+            speed = jnp.where(freq_of_lane == c, courant_ref[c * FCHUNK + fi], speed)
         for side in range(2):
-            field = acc[side] * sea_pair[side]
+            field = acc[side * FCHUNK + fi] * sea_pair[side]
             upwind = pltpu.roll(field, 1 if side == 0 else 127, 1)
             south = jnp.where(row == 0, 0.0, pltpu.roll(field, 1, 0))
             north = jnp.where(row == 7, 0.0, pltpu.roll(field, 7, 0))
@@ -156,10 +161,7 @@
                 both = jnp.where(odd, later, pltpu.roll(field, 127, 1))
             else:
                 both = jnp.where(odd, pltpu.roll(field, 1, 1), later)
-            pack[side, g] = both
-        return carry
-
-    lax.fori_loop(0, chunks, chunk, 0)
+            pack[side, fi] = both
 
     to_east = pltpu.make_async_remote_copy(
         src_ref=pack.at[0],
@@ -272,30 +274,32 @@
     first, last = lane == 0, lane == 127
     bottom, top = row == 0, row == 7
 
-    def propagate(g, energy):
-        load(g).wait()
+    def propagate(c, energy):
+        load(c).wait()
         sums = [energy] + [jnp.zeros((8, 128), jnp.float32) for _ in range(3)]
-        halos = (west_ref[g], east_ref[g])
-        turn = 0
-        for fi in range(FCHUNK):
-            f = g * FCHUNK + fi
-            speed = courant_ref[f]
+        speeds = [courant_ref[c * FCHUNK + fi] for fi in range(FCHUNK)]
+        for k in range(max(len(forward), len(backward))):
             for side, members in enumerate((forward, backward)):
-                for k, d in enumerate(members):
-                    at = fi * slots + 2 * k
-                    halo = pltpu.roll(halos[side], (127 - at) % 128, 1)
-                    step_x = speed * float(abs(cosine[d]))
-                    step_y = speed * float(abs(sine[d]))
+                if k >= len(members):
+                    continue
+                d = members[k]
+                halo_ref = (west_ref, east_ref)[side]
+                turn = 127 - 2 * k - c * slots
+                halos = [pltpu.roll(halo_ref[fi], turn, 1) for fi in range(FCHUNK)]
+                shift = 1 if side == 0 else 127
+                done = []
+                for fi in range(FCHUNK):
+                    step_x = speeds[fi] * float(abs(cosine[d]))
+                    step_y = speeds[fi] * float(abs(sine[d]))
                     keep = 1.0 - step_x - step_y
-                    shift = 1 if side == 0 else 127
-                    field = spec[f, d] * sea
+                    field = spec[c * FCHUNK + fi, d] * sea
                     for substep in range(2):
                         if substep == 0:
-                            upwind = jnp.where(last if side == 0 else first, halo, field)
+                            upwind = jnp.where(last if side == 0 else first, halos[fi], field)
                             upwind = pltpu.roll(upwind, shift, 1)
                         else:
                             upwind = pltpu.roll(field, shift, 1)
-                            upwind = jnp.where(first if side == 0 else last, halo, upwind)
+                            upwind = jnp.where(first if side == 0 else last, halos[fi], upwind)
                         result = keep * field + step_x * upwind
                         if sine[d] != 0:
                             up = sine[d] > 0
@@ -303,9 +307,10 @@
                             beside = jnp.where(bottom if up else top, 0.0, beside)
                             result = result + step_y * beside
                         field = sea * result
-                    out[f, d] = field
-                    sums[turn % 4] = sums[turn % 4] + field
-                    turn += 1
+                    done.append(field)
+                for fi, field in enumerate(done):
+                    out[c * FCHUNK + fi, d] = field
+                    sums[fi % 4] = sums[fi % 4] + field
         return (sums[0] + sums[1]) + (sums[2] + sums[3])
 
     energy = lax.fori_loop(0, chunks, propagate, jnp.zeros((8, 128), jnp.float32))
@@ -430,13 +435,13 @@
     bands = ranks // ATY
     f32 = jnp.float32
     _, _, forward, _ = directions(dirs)
-    consts = jnp.asarray(pack_constants(dirs, 2 * len(forward)))
-    anywhere = pl.BlockSpec(memory_space=pl.ANY)
+    consts = jnp.asarray(pack_constants(dirs, 2 * len(forward), chunks))
+    anywhere = pl.BlockSpec(memory_space=pltpu.HBM)
     vmem = pl.BlockSpec(memory_space=pltpu.VMEM)
     smem = pl.BlockSpec(memory_space=pltpu.SMEM)
     dma = pltpu.SemaphoreType.DMA
     span = atmos_fields.shape[3] // ATY
-    halo = jax.ShapeDtypeStruct((chunks, lat, width), f32)
+    halo = jax.ShapeDtypeStruct((FCHUNK, lat, width), f32)
     table, west, east = pl.pallas_call(
         functools.partial(exchange_kernel, ranks),
         out_shape=(
@@ -448,7 +453,7 @@
         out_specs=(anywhere, anywhere, anywhere),
         scratch_shapes=[
             pltpu.VMEM(spectrum.shape, f32),
-            pltpu.VMEM((2, chunks, lat, width), f32),
+            pltpu.VMEM((2, FCHUNK, lat, width), f32),
             dma((chunks,)),
             dma((ATY,)),
             dma((ATY,)),
@@ -456,7 +461,7 @@
             dma((2,)),
         ],
         compiler_params=pltpu.CompilerParams(
-            collective_id=0, has_side_effects=True, vmem_limit_bytes=16 * 2**20
+            collective_id=0, has_side_effects=True, vmem_limit_bytes=62 * 2**20
         ),
         name="exchange",
     )(spectrum, sea_mask, courant, consts, atmos_fields)
@@ -478,7 +483,7 @@
             dma((chunks,)),
             dma((chunks,)),
         ],
-        compiler_params=pltpu.CompilerParams(vmem_limit_bytes=24 * 2**20),
+        compiler_params=pltpu.CompilerParams(vmem_limit_bytes=62 * 2**20),
         name="wave",
     )(
         spectrum,
@@ -505,7 +510,7 @@
             dma((ATY,)),
             dma((ATY,)),
         ],
-        compiler_params=pltpu.CompilerParams(collective_id=1, has_side_effects=True),
+        compiler_params=pltpu.CompilerParams(collective_id=1, has_side_effects=True, vmem_limit_bytes=62 * 2**20),
         name="give_back",
     )(stress)
     return (updated, roughness)

time: 56 us -> 35.6 us (0.64)
  Pallas kernels: 48.1 us -> 33.2 us
  local copies, waits for them, and re-layouts: 6.7 us -> 1.32 us
    pallas_call x1, Pallas kernels: 29.4 us -> 15.8 us  [on_device(): pl.pallas_call(functools.partial(wave_kernel, bands), out_shape=(jax.Shap...]
    unnamed x31 -> x1, local copies, waits for them, and re-layouts: 6.7 us -> 1.32 us
    pallas_call x1, Pallas kernels: 12.5 us -> 10.6 us  [on_device(): pl.pallas_call(functools.partial(exchange_kernel, ranks), out_shape=(jax....]
    pallas_call x1, Pallas kernels: 6.2 us -> 6.86 us  [on_device(): pl.pallas_call(functools.partial(return_kernel, ranks), out_shape=jax.Sha...]
where the time goes in v2:
time: 35.6 us; the launch traced here: 35.2 us
  Pallas kernels  33.2 us (93%)
  local copies, waits for them, and re-layouts  1.32 us (4%)
  between operations  0.65 us (2%)
    pallas_call x1, Pallas kernels, on_device(): pl.pallas_call(functools.partial(wave_kernel, bands), out_shape=(jax.Shap...  15.8 us
    pallas_call x1, Pallas kernels, on_device(): pl.pallas_call(functools.partial(exchange_kernel, ranks), out_shape=(jax....  10.6 us
    pallas_call x1, Pallas kernels, on_device(): pl.pallas_call(functools.partial(return_kernel, ranks), out_shape=jax.Sha...  6.86 us
    unnamed x1, local copies, waits for them, and re-layouts  1.32 us

profile of v2, /device:TPU:0, one launch (start us, length us, event | category | flops | bytes accessed | tf_op | source)
XLA Modules:
  0.0 35.2 jit_solution(3424802127009288330)
XLA Ops:
  0.6 10.6 %exchange.1 = (f32[4,4,4,256]{3,2,1,0:T(4,128)}, f32[6,8,128]{2,1,0:T(8,128)}, f32[6,8,128]{2,1,0:T(8,128)}) custom-call(f32[30,24,8,128]{3,2,1,0:T(8,128)} %spec_hbm.3, s32[8,128]{1,0:T(8,128)} %sea_ref.3, f32[30]{0:T(128)} %courant_ref.3, f32[2,3,8,128]{3,2,1,0:T(8,128)} %constant.2.clone.const_ref, f32[1,4,4,1024]{3,2,1,0:T(4,128)} %atmos_ref.1), custom_call_target="tpu_custom_call" | custom-call | tf_op jit(solution)/shard_map/exchange/pallas_call | solution.py:445
  11.2 15.8 %wave.1 = (f32[30,24,8,128]{3,2,1,0:T(8,128)}, f32[32,128]{1,0:T(8,128)}) custom-call(f32[30,24,8,128]{3,2,1,0:T(8,128)} %spec_hbm.3, s32[8,128]{1,0:T(8,128)} %sea_ref.3, f32[30]{0:T(128)} %courant_ref.3, f32[30]{0:T(128)} %phase_ref.1, f32[30]{0:T(128)} %rate_ref.1, f32[30]{0:T(128)} %decay_ref.1, s32[4,8,128]{2,1,0:T(8,128)} %tile_ref.1, ...), custom_call_target="tpu_custom_call" | custom-call | tf_op jit(solution)/shard_map/wave/pallas_call | solution.py:469
  27.0 6.9 %give_back.1 = f32[1,4,1024]{2,1,0:T(4,128)} custom-call(f32[32,128]{1,0:T(8,128)} %get-tuple-element.11.stress_ref), custom_call_target="tpu_custom_call" | custom-call | tf_op jit(solution)/shard_map/give_back/pallas_call | solution.py:503
  33.9 1.3 %copy.14 = f32[1,4,1024]{2,1,0:T(4,128)} copy(f32[1,4,1024]{2,1,0:T(4,128)} %give_back.1) | data formatting | bytes 32768

commit v3 on v2

--- a/solution.py
+++ b/solution.py
@@ -52,6 +52,7 @@
     west_ref,
     east_ref,
     spec,
+    stage,
     pack,
     in_sem,
     piece_send,
@@ -128,22 +129,29 @@
     sea_pair = (tiled(2), tiled(0))
     freq_of_lane = lane // slots
 
-    def chunk(c, acc):
+    blank = jnp.zeros((8, 128), jnp.float32)
+    for c in range(chunks):
         load(c).wait()
-        acc = list(acc)
-        for m in range(len(forward) + 1):
-            for side, members, k in ((0, forward, m - 1), (1, backward, m)):
-                if not 0 <= k < len(members):
-                    continue
-                here = half == c * (slots // 2) + k
+    for m in range(len(forward) + 1):
+        for side, members, k in ((0, forward, m - 1), (1, backward, m)):
+            if not 0 <= k < len(members):
+                continue
+            here = half == k
+            for c in range(chunks):
+                merged = []
                 for fi in range(FCHUNK):
-                    value = pltpu.roll(spec[c * FCHUNK + fi, members[k]], c * slots + 2 * m, 1)
-                    at = side * FCHUNK + fi
-                    acc[at] = jnp.where(here, value, acc[at])
-        return tuple(acc)
-
-    blank = jnp.zeros((8, 128), jnp.float32)
-    acc = lax.fori_loop(0, chunks, chunk, (blank,) * (2 * FCHUNK))
+                    value = spec[c * FCHUNK + fi, members[k]]
+                    if m:
+                        value = pltpu.roll(value, 2 * m, 1)
+                    before = blank if k == 0 else stage[side, c * FCHUNK + fi]
+                    merged.append(jnp.where(here, value, before))
+                for fi in range(FCHUNK):
+                    stage[side, c * FCHUNK + fi] = merged[fi]
+    acc = [stage[n // FCHUNK, n % FCHUNK] for n in range(2 * FCHUNK)]
+    for c in range(1, chunks):
+        for n in range(2 * FCHUNK):
+            value = stage[n // FCHUNK, c * FCHUNK + n % FCHUNK]
+            acc[n] = acc[n] + pltpu.roll(value, c * slots, 1)
     for fi in range(FCHUNK):
         speed = blank
         for c in range(chunks):
@@ -212,6 +220,7 @@
     stress_ref,
     spec,
     out,
+    stage,
     along_ref,
     lane_hot,
     row_hot,
@@ -274,32 +283,48 @@
     first, last = lane == 0, lane == 127
     bottom, top = row == 0, row == 7
 
+    sides = ((forward, west_ref), (backward, east_ref))
+    for c in range(chunks):
+        for side in range(2):
+            for fi in range(FCHUNK):
+                halo = sides[side][1][fi]
+                if c:
+                    halo = pltpu.roll(halo, 128 - c * slots, 1)
+                stage[side, c * FCHUNK + fi] = halo
+    for k in range(len(forward)):
+        for side in range(2):
+            members = sides[side][0]
+            if k >= len(members):
+                continue
+            for c in range(chunks):
+                rolled = [
+                    pltpu.roll(stage[side, c * FCHUNK + fi], 127 - 2 * k, 1)
+                    for fi in range(FCHUNK)
+                ]
+                for fi in range(FCHUNK):
+                    out[c * FCHUNK + fi, members[k]] = rolled[fi]
+
     def propagate(c, energy):
         load(c).wait()
         sums = [energy] + [jnp.zeros((8, 128), jnp.float32) for _ in range(3)]
         speeds = [courant_ref[c * FCHUNK + fi] for fi in range(FCHUNK)]
-        for k in range(max(len(forward), len(backward))):
-            for side, members in enumerate((forward, backward)):
-                if k >= len(members):
-                    continue
-                d = members[k]
-                halo_ref = (west_ref, east_ref)[side]
-                turn = 127 - 2 * k - c * slots
-                halos = [pltpu.roll(halo_ref[fi], turn, 1) for fi in range(FCHUNK)]
-                shift = 1 if side == 0 else 127
+        for side, members in enumerate((forward, backward)):
+            shift = 1 if side == 0 else 127
+            for d in members:
                 done = []
                 for fi in range(FCHUNK):
                     step_x = speeds[fi] * float(abs(cosine[d]))
                     step_y = speeds[fi] * float(abs(sine[d]))
                     keep = 1.0 - step_x - step_y
+                    halo = out[c * FCHUNK + fi, d]
                     field = spec[c * FCHUNK + fi, d] * sea
                     for substep in range(2):
                         if substep == 0:
-                            upwind = jnp.where(last if side == 0 else first, halos[fi], field)
+                            upwind = jnp.where(last if side == 0 else first, halo, field)
                             upwind = pltpu.roll(upwind, shift, 1)
                         else:
                             upwind = pltpu.roll(field, shift, 1)
-                            upwind = jnp.where(first if side == 0 else last, halos[fi], upwind)
+                            upwind = jnp.where(first if side == 0 else last, halo, upwind)
                         result = keep * field + step_x * upwind
                         if sine[d] != 0:
                             up = sine[d] > 0
@@ -453,6 +478,7 @@
         out_specs=(anywhere, anywhere, anywhere),
         scratch_shapes=[
             pltpu.VMEM(spectrum.shape, f32),
+            pltpu.VMEM((2, freqs, lat, width), f32),
             pltpu.VMEM((2, FCHUNK, lat, width), f32),
             dma((chunks,)),
             dma((ATY,)),
@@ -477,6 +503,7 @@
         scratch_shapes=[
             pltpu.VMEM(spectrum.shape, f32),
             pltpu.VMEM(spectrum.shape, f32),
+            pltpu.VMEM((2, freqs, lat, width), f32),
             pltpu.VMEM((dirs, lat, width), f32),
             pltpu.VMEM((128, 32 * 128), jnp.bfloat16),
             pltpu.VMEM((96, 32 * 128), jnp.bfloat16),
@@ -503,7 +530,7 @@
     roughness = pl.pallas_call(
         functools.partial(return_kernel, ranks),
         out_shape=jax.ShapeDtypeStruct((1,) + atmos_fields.shape[2:], f32),
-        in_specs=[vmem],
+        in_specs=[anywhere],
         out_specs=vmem,
         scratch_shapes=[
             pltpu.VMEM((ATY, 8, 128), f32),

time: 35.6 us -> 27.8 us (0.78)
  Pallas kernels: 33.2 us -> 25.5 us
    pallas_call x1, Pallas kernels: 15.8 us -> 8.56 us  [on_device(): pl.pallas_call(functools.partial(wave_kernel, bands), out_shape=(jax.Shap...]
    pallas_call x1, Pallas kernels: 6.86 us -> 6.2 us  [on_device(): pl.pallas_call(functools.partial(return_kernel, ranks), out_shape=jax.Sha...]
where the time goes in v3:
time: 27.8 us; the launch traced here: 27.5 us
  Pallas kernels  25.5 us (92%)
  local copies, waits for them, and re-layouts  1.32 us (5%)
  between operations  0.65 us (2%)
    pallas_call x1, Pallas kernels, on_device(): pl.pallas_call(functools.partial(exchange_kernel, ranks), out_shape=(jax....  10.8 us
    pallas_call x1, Pallas kernels, on_device(): pl.pallas_call(functools.partial(wave_kernel, bands), out_shape=(jax.Shap...  8.56 us
    pallas_call x1, Pallas kernels, on_device(): pl.pallas_call(functools.partial(return_kernel, ranks), out_shape=jax.Sha...  6.2 us
    unnamed x1, local copies, waits for them, and re-layouts  1.32 us

profile of v3, /device:TPU:0, one launch (start us, length us, event | category | flops | bytes accessed | tf_op | source)
XLA Modules:
  0.0 27.5 jit_solution(5011920641340277659)
XLA Ops:
  0.6 10.8 %exchange.1 = (f32[4,4,4,256]{3,2,1,0:T(4,128)}, f32[6,8,128]{2,1,0:T(8,128)}, f32[6,8,128]{2,1,0:T(8,128)}) custom-call(f32[30,24,8,128]{3,2,1,0:T(8,128)} %spec_hbm.3, s32[8,128]{1,0:T(8,128)} %sea_ref.3, f32[30]{0:T(128)} %courant_ref.3, f32[2,3,8,128]{3,2,1,0:T(8,128)} %constant.2.clone.const_ref, f32[1,4,4,1024]{3,2,1,0:T(4,128)} %atmos_ref.1), custom_call_target="tpu_custom_call" | custom-call | tf_op jit(solution)/shard_map/exchange/pallas_call | solution.py:470
  11.4 8.6 %wave.1 = (f32[30,24,8,128]{3,2,1,0:T(8,128)}, f32[32,128]{1,0:T(8,128)}) custom-call(f32[30,24,8,128]{3,2,1,0:T(8,128)} %spec_hbm.3, s32[8,128]{1,0:T(8,128)} %sea_ref.3, f32[30]{0:T(128)} %courant_ref.3, f32[30]{0:T(128)} %phase_ref.1, f32[30]{0:T(128)} %rate_ref.1, f32[30]{0:T(128)} %decay_ref.1, s32[4,8,128]{2,1,0:T(8,128)} %tile_ref.1, ...), custom_call_target="tpu_custom_call" | custom-call | tf_op jit(solution)/shard_map/wave/pallas_call | solution.py:495
  20.0 6.2 %give_back.1 = f32[1,4,1024]{2,1,0:T(4,128)} custom-call(f32[32,128]{1,0:T(8,128)} %get-tuple-element.11.stress_ref), custom_call_target="tpu_custom_call" | custom-call | tf_op jit(solution)/shard_map/give_back/pallas_call | solution.py:530
  26.2 1.3 %copy.14 = f32[1,4,1024]{2,1,0:T(4,128)} copy(f32[1,4,1024]{2,1,0:T(4,128)} %give_back.1) | data formatting | bytes 32768

commit v4 on v3

--- a/solution.py
+++ b/solution.py
@@ -88,8 +88,6 @@
         def _():
             pl.semaphore_signal(barrier, inc=1, device_id={"gx": source}, device_id_type=MESH)
 
-    pl.semaphore_wait(barrier, 2 + ATY - own.astype(jnp.int32))
-
     span = atmos_ref.shape[3] // ATY
 
     def piece(j):
@@ -105,15 +103,18 @@
             device_id_type=MESH,
         )
 
-    for j in range(ATY):
-
-        @pl.when(first_target + j != me)
-        def _():
-            piece_copy(j).start()
-
-        @pl.when(first_target + j == me)
-        def _():
-            pltpu.make_async_copy(piece(j), table_ref.at[band], piece_recv.at[band]).start()
+    def send_pieces():
+        pl.semaphore_wait(barrier, 2 + ATY - own.astype(jnp.int32))
+
+        for j in range(ATY):
+
+            @pl.when(first_target + j != me)
+            def _():
+                piece_copy(j).start()
+
+            @pl.when(first_target + j == me)
+            def _():
+                pltpu.make_async_copy(piece(j), table_ref.at[band], piece_recv.at[band]).start()
 
     lane, row = lane_row((8, 128))
     half = lane // 2
@@ -133,6 +134,8 @@
     for c in range(chunks):
         load(c).wait()
     for m in range(len(forward) + 1):
+        if m == len(forward) // 2:
+            send_pieces()
         for side, members, k in ((0, forward, m - 1), (1, backward, m)):
             if not 0 <= k < len(members):
                 continue

time: 27.8 us -> 28.3 us (1.018)
  Pallas kernels: 25.5 us -> 26 us
    pallas_call x1, Pallas kernels: 6.2 us -> 6.53 us  [on_device(): pl.pallas_call(functools.partial(return_kernel, ranks), out_shape=jax.Sha...]
where the time goes in v4:
time: 28.3 us; the launch traced here: 28 us
  Pallas kernels  26 us (92%)
  local copies, waits for them, and re-layouts  1.32 us (5%)
  between operations  0.65 us (2%)
    pallas_call x1, Pallas kernels, on_device(): pl.pallas_call(functools.partial(exchange_kernel, ranks), out_shape=(jax....  10.9 us
    pallas_call x1, Pallas kernels, on_device(): pl.pallas_call(functools.partial(wave_kernel, bands), out_shape=(jax.Shap...  8.56 us
    pallas_call x1, Pallas kernels, on_device(): pl.pallas_call(functools.partial(return_kernel, ranks), out_shape=jax.Sha...  6.53 us
    unnamed x1, local copies, waits for them, and re-layouts  1.32 us

profile of v4, /device:TPU:0, one launch (start us, length us, event | category | flops | bytes accessed | tf_op | source)
XLA Modules:
  0.0 28.0 jit_solution(9640980188349785429)
XLA Ops:
  0.6 10.9 %exchange.1 = (f32[4,4,4,256]{3,2,1,0:T(4,128)}, f32[6,8,128]{2,1,0:T(8,128)}, f32[6,8,128]{2,1,0:T(8,128)}) custom-call(f32[30,24,8,128]{3,2,1,0:T(8,128)} %spec_hbm.3, s32[8,128]{1,0:T(8,128)} %sea_ref.3, f32[30]{0:T(128)} %courant_ref.3, f32[2,3,8,128]{3,2,1,0:T(8,128)} %constant.2.clone.const_ref, f32[1,4,4,1024]{3,2,1,0:T(4,128)} %atmos_ref.1), custom_call_target="tpu_custom_call" | custom-call | tf_op jit(solution)/shard_map/exchange/pallas_call | solution.py:473
  11.5 8.6 %wave.1 = (f32[30,24,8,128]{3,2,1,0:T(8,128)}, f32[32,128]{1,0:T(8,128)}) custom-call(f32[30,24,8,128]{3,2,1,0:T(8,128)} %spec_hbm.3, s32[8,128]{1,0:T(8,128)} %sea_ref.3, f32[30]{0:T(128)} %courant_ref.3, f32[30]{0:T(128)} %phase_ref.1, f32[30]{0:T(128)} %rate_ref.1, f32[30]{0:T(128)} %decay_ref.1, s32[4,8,128]{2,1,0:T(8,128)} %tile_ref.1, ...), custom_call_target="tpu_custom_call" | custom-call | tf_op jit(solution)/shard_map/wave/pallas_call | solution.py:498
  20.1 6.5 %give_back.1 = f32[1,4,1024]{2,1,0:T(4,128)} custom-call(f32[32,128]{1,0:T(8,128)} %get-tuple-element.11.stress_ref), custom_call_target="tpu_custom_call" | custom-call | tf_op jit(solution)/shard_map/give_back/pallas_call | solution.py:533
  26.6 1.3 %copy.14 = f32[1,4,1024]{2,1,0:T(4,128)} copy(f32[1,4,1024]{2,1,0:T(4,128)} %give_back.1) | data formatting | bytes 32768
